TPU v7x, 128 devices: a whole 4x4x4 slice. The times are simulated.
128 devices in a mesh: row: 8 (over y, core), col: 16 (over z, x).
Axes of the slice: x: 4, y: 4, z: 4, core: 2. Of those that a mesh axis runs over, the one named last changes fastest.
Arguments:
- user_factors: float32 [16384, 128], P('row'), may hold values from -6 to 6
- item_factors: float32 [131072, 128], P(('row', 'col')), may hold values from -0.015625 to 0.015625
- fetch_list: int32 [8, 16, 128, 1], P('row', 'col'), may hold values from 0 to 7
- tile_user: int32 [8, 16, 32], P('row', 'col'), may hold values from 0 to 15
- tile_slot: int32 [8, 16, 32], P('row', 'col'), may hold values from 0 to 127
- entry_row: int32 [8, 16, 32, 512], P('row', 'col'), may hold values from 0 to 127
- entry_col: int32 [8, 16, 32, 512], P('row', 'col'), may hold values from 0 to 127
- entry_count: int32 [8, 16, 32, 512], P('row', 'col'), may hold values from 1 to 8
- tile_count: int32 [8, 16], P('row', 'col'), may hold values from 4 to 32, as said below
Outputs:
- solved: float32 [16384, 128], P('row')
Inputs may be any that keep to these rules, and one draw needn't show every extreme that they name: `tile_count`: at least 4 tiles live on every device; some device has all 32 live in every draw.
All inputs are finite; a program needn't handle non-finite values.
Results may differ from a plain program's by a relative error of at most 0.0003.
Values sent between devices are 32-bit elements; how exact they have to be, the bound alone decides.
A program may use at most 128 MiB of HBM per device.

v0:
```python
import jax
import jax.numpy as jnp
from jax import lax
from jax.sharding import PartitionSpec as P

K = 128
BLOCK = 128
ITERS = 3
HIGHEST = lax.Precision.HIGHEST
CONFIDENCE_SCALE = 40.0
RIDGE = 0.5
EPSILON = 1e-06


def conjugate(iterate, residual, apply_full):
    direction = residual
    norm_now = jnp.sum(residual * residual, axis=1, keepdims=True)
    for iteration in range(ITERS):
        image = apply_full(direction)
        alpha = norm_now / (jnp.sum(direction * image, axis=1, keepdims=True) + EPSILON)
        iterate = iterate + alpha * direction
        residual = residual - alpha * image
        norm_next = jnp.sum(residual * residual, axis=1, keepdims=True)
        direction = residual + norm_next / (norm_now + EPSILON) * direction
        norm_now = norm_next
    return iterate


def shards(
    user_factors,
    item_factors,
    fetch_list,
    tile_user,
    tile_slot,
    entry_row,
    entry_col,
    entry_count,
    tile_count,
):
    user_rows = user_factors.shape[0]
    user_blocks = user_rows // BLOCK
    local_blocks = item_factors.reshape(-1, BLOCK, K)
    wanted = fetch_list[0, 0]
    peers = wanted.shape[0]
    width = wanted.shape[1]
    asked = lax.all_to_all(wanted, ("row", "col"), split_axis=0, concat_axis=0, tiled=True)
    served = jnp.take(local_blocks, asked.reshape(-1), axis=0).reshape(peers, width, BLOCK, K)
    fetched = lax.all_to_all(
        served, ("row", "col"), split_axis=0, concat_axis=0, tiled=True
    ).reshape(-1, BLOCK, K)
    gram = lax.psum(
        jnp.dot(
            item_factors.T, item_factors, precision=HIGHEST, preferred_element_type=jnp.float32
        ),
        ("row", "col"),
    )
    users = tile_user[0, 0]
    slot_ids = tile_slot[0, 0]
    tiles = users.shape[0]
    tile_index = jnp.arange(tiles, dtype=jnp.int32)
    alive = (tile_index < tile_count[0, 0]).astype(jnp.float32)
    excess = CONFIDENCE_SCALE * entry_count[0, 0].astype(jnp.float32)
    weight_fit = excess * alive[:, None]
    weight_rhs = (1.0 + excess) * alive[:, None]
    rows_in = entry_row[0, 0]
    cols_in = entry_col[0, 0]
    block_ids = jnp.arange(BLOCK, dtype=jnp.int32)
    row_onehot = (rows_in[:, :, None] == block_ids[None, None, :]).astype(jnp.float32)
    col_onehot = (cols_in[:, :, None] == block_ids[None, None, :]).astype(jnp.float32)
    dense_fit = jnp.einsum(
        "tnu,tni->tui", row_onehot * weight_fit[:, :, None], col_onehot, precision=HIGHEST
    )
    dense_rhs = jnp.einsum(
        "tnu,tni->tui", row_onehot * weight_rhs[:, :, None], col_onehot, precision=HIGHEST
    )
    item_tiles = jnp.take(fetched, slot_ids, axis=0)
    owner_onehot = (users[None, :] == jnp.arange(user_blocks, dtype=jnp.int32)[:, None]).astype(
        jnp.float32
    )

    def tile_terms(vector):
        picked_users = jnp.take(vector.reshape(user_blocks, BLOCK, K), users, axis=0)
        scores = jnp.einsum("tuk,tik->tui", picked_users, item_tiles, precision=HIGHEST)
        pulled = jnp.einsum("tui,tik->tuk", dense_fit * scores, item_tiles, precision=HIGHEST)
        return jnp.einsum("bt,tuk->buk", owner_onehot, pulled, precision=HIGHEST).reshape(
            user_rows, K
        )

    rhs_pulled = jnp.einsum("tui,tik->tuk", dense_rhs, item_tiles, precision=HIGHEST)
    rhs_local = jnp.einsum("bt,tuk->buk", owner_onehot, rhs_pulled, precision=HIGHEST).reshape(
        user_rows, K
    )

    def extra(vector):
        return (
            jnp.dot(vector, gram, precision=HIGHEST, preferred_element_type=jnp.float32)
            + RIDGE * vector
        )

    start_terms = rhs_local - tile_terms(user_factors)

    def apply_whole(vector):
        return lax.psum(tile_terms(vector), "col") + extra(vector)

    residual = lax.psum(start_terms, "col") - extra(user_factors)
    solved = conjugate(user_factors, residual, apply_whole)
    return solved


def solution(mesh):
    return jax.shard_map(
        shards,
        mesh=mesh,
        in_specs=(
            P("row", None),
            P(("row", "col"), None),
            P("row", "col", None, None),
            P("row", "col", None),
            P("row", "col", None),
            P("row", "col", None, None),
            P("row", "col", None, None),
            P("row", "col", None, None),
            P("row", "col"),
        ),
        out_specs=P("row", None),
        check_vma=False,
    )
```

profile of v0, /device:TPU:0, one launch (start us, length us, event | category | flops | bytes accessed | tf_op | source)
XLA Modules:
  0.0 695.5 jit_solution(1226374862709490610)
XLA Ops:
  7.4 20.4 %all_to_all.20 = s32[128,1,1]{2,1,0:T(1,128)S(1)} all-to-all(s32[128,1,1]{2,1,0:T(1,128)S(1)} %copy.50), channel_id=1, replica_groups=mesh['row'=8,'col'=16] {'row','col'}, dimensions={0} | all-to-all | bytes 1024 | tf_op jit(solution)/shard_map/all_to_all | solution.py:46
  30.2 4.3 gather_fusion
  34.5 7.2 %bitcast_select_fusion = f32[128,1,128,128]{3,2,1,0:T(8,128)} fusion(f32[128,128,128]{2,1,0:T(8,128)} %gather_fusion, pred[128]{0:T(512)(128)(4,1)S(1)} %compare_and_fusion.1), kind=kLoop, calls=%fused_computation.6 | loop fusion | flops 2097152 | bytes 16777344 | tf_op jit(solution)/shard_map/jit(_take)/select_n | solution.py:47
  41.7 6.1 all-to-all-start.1
  52.4 8.1 %fusion = f32[32,128,128]{2,1,0:T(8,128)} fusion(f32[32,512]{1,0:T(8,128)S(1)} %get-tuple-element.11, s32[32,512]{1,0:T(8,128)S(1)} %bitcast.99, s32[32,512]{1,0:T(8,128)S(1)} %bitcast.101), kind=kOutput, calls=%fused_computation.7 | convolution fusion | flops 3227516928 | bytes 2293760 | tf_op jit(solution)/shard_map/tnu,tni->tui/dot_general | solution.py:70
  60.5 8.2 %fusion.2 = f32[32,128,128]{2,1,0:T(8,128)} fusion(s32[32,512]{1,0:T(8,128)S(1)} %bitcast.100, f32[32,512]{1,0:T(8,128)S(1)} %get-tuple-element.10, s32[32,512]{1,0:T(8,128)S(1)} %bitcast.102), kind=kOutput, calls=%fused_computation.10 | convolution fusion | flops 3227516928 | bytes 2293760 | tf_op jit(solution)/shard_map/tnu,tni->tui/dot_general | solution.py:73
  68.8 79.1 %all-to-all-done.1 = f32[128,1,128,128]{3,2,1,0:T(8,128)} async-done(((f32[128,1,128,128]{3,2,1,0:T(8,128)}), f32[128,1,128,128]{3,2,1,0:T(8,128)}, u32[]{:S(2)}, u32[]{:S(2)}) %all-to-all-start.1) | async-done | bytes 8388640 | tf_op jit(solution)/shard_map/all_to_all | solution.py:48
  147.9 4.1 gather_fusion.1
  152.0 3.9 fusion.50
  155.9 4.6 fusion.28
  168.4 2.6 copy.54
  172.3 81.8 %all-reduce.8.cloned.1.call-done = f32[128,128]{1,0:T(8,128)} async-done(((f32[128,128]{1,0:T(8,128)}), f32[128,128]{1,0:T(8,128)}) %all-reduce.8.cloned.1.call-update) | async-done | bytes 65552 | tf_op jit(solution)/shard_map/psum | solution.py:51
  254.1 90.1 %all-reduce.6.cloned.1.call-done = f32[2048,128]{0,1:T(8,128)} async-done(((f32[2048,128]{0,1:T(8,128)}), f32[2048,128]{0,1:T(8,128)}) %all-reduce.6.cloned.1.call-update) | async-done | bytes 1048592 | tf_op jit(solution)/shard_map/psum | solution.py:105
  344.2 3.0 fusion.13
  348.5 3.2 gather_fusion.3
  351.7 6.3 fusion.26
  358.0 3.6 fusion.34
  361.7 3.1 copy.69
  369.0 86.0 %all-reduce.10.cloned.1.call-done = f32[2048,128]{0,1:T(8,128)} async-done(((f32[2048,128]{0,1:T(8,128)}), f32[2048,128]{0,1:T(8,128)}) %all-reduce.10.cloned.1.call-update) | async-done | bytes 1048592 | tf_op jit(solution)/shard_map/psum | solution.py:103
  459.9 2.6 copy.79
  462.4 3.2 gather_fusion.4
  465.6 6.3 fusion.24
  472.0 3.6 fusion.32
  475.6 3.1 copy.72
  482.7 86.2 %all-reduce.12.cloned.1.call-done = f32[2048,128]{0,1:T(8,128)} async-done(((f32[2048,128]{0,1:T(8,128)}), f32[2048,128]{0,1:T(8,128)}) %all-reduce.12.cloned.1.call-update) | async-done | bytes 1048592 | tf_op jit(solution)/shard_map/psum | solution.py:103
  568.8 3.2 multiply_reduce_fusion.1
  576.1 3.2 gather_fusion.5
  579.3 6.3 fusion.22
  585.6 3.6 fusion.30
  593.8 86.4 %all-reduce.14.cloned.1.call-done = f32[2048,128]{0,1:T(8,128)} async-done(((f32[2048,128]{0,1:T(8,128)}), f32[2048,128]{0,1:T(8,128)}) %all-reduce.14.cloned.1.call-update) | async-done | bytes 1048592 | tf_op jit(solution)/shard_map/psum | solution.py:103
  680.2 3.0 fusion.41
  683.3 3.0 multiply_add_fusion
  (86 shorter events, 41.7 us)
Async XLA Ops:
  6.5 23.6 %copy-start = (f32[1024,128]{1,0:T(8,128)S(1)}, f32[1024,128]{1,0:T(8,128)}, u32[]{:S(2)}) copy-start(f32[1024,128]{1,0:T(8,128)} %param.12) | copy-start | bytes 1572868
  41.7 8.5 %copy-start.14 = (s32[1,1,32]{2,1,0:T(1,128)S(1)}, s32[1,1,32]{2,1,0:T(1,128)}, u32[]{:S(2)}) copy-start(s32[1,1,32]{2,1,0:T(1,128)} %param.14) | copy-start | bytes 388
  41.7 106.2 %all-to-all-start.1 = ((f32[128,1,128,128]{3,2,1,0:T(8,128)}), f32[128,1,128,128]{3,2,1,0:T(8,128)}, u32[]{:S(2)}, u32[]{:S(2)}) async-start(f32[128,1,128,128]{3,2,1,0:T(8,128)} %bitcast_select_fusion), calls=%async_computation.1 | async-start | bytes 16777216 | tf_op jit(solution)/shard_map/all_to_all | solution.py:48
  47.8 2.5 copy-start.10
  47.8 206.3 %all-reduce.8.cloned.1.call-start = ((), (), s32[]{:S(2)}) async-start(), calls=%async_computation.3 | async-start | bytes 131072 | tf_op jit(solution)/shard_map/psum | solution.py:51
  49.5 294.7 %all-reduce.6.cloned.1.call-start = ((), (), s32[]{:S(2)}) async-start(), calls=%async_computation.2 | async-start | bytes 2097152 | tf_op jit(solution)/shard_map/psum | solution.py:105
  50.2 2.0 copy-start.15
  50.3 2.1 copy-start.13
  50.3 2.2 copy-start.16
  50.3 2.2 copy-start.17
  151.9 4.0 copy-start.11
  155.9 4.6 copy-start.2
  171.0 284.0 %all-reduce.10.cloned.1.call-start = ((), (), s32[]{:S(2)}) async-start(), calls=%async_computation.4 | async-start | bytes 2097152 | tf_op jit(solution)/shard_map/psum | solution.py:103
  351.7 6.3 copy-start.3
  367.2 87.8 %copy-start.12 = (f32[128,128]{1,0:T(8,128)S(1)}, f32[128,128]{1,0:T(8,128)}, u32[]{:S(2)}) copy-start(f32[128,128]{1,0:T(8,128)} %all-reduce.8.cloned.1.call-done) | copy-start | bytes 196612
  368.5 200.3 %all-reduce.12.cloned.1.call-start = ((), (), s32[]{:S(2)}) async-start(), calls=%async_computation.5 | async-start | bytes 2097152 | tf_op jit(solution)/shard_map/psum | solution.py:103
  457.7 1.0 copy-start.8
  465.6 6.3 copy-start.4
  482.4 197.8 %all-reduce.14.cloned.1.call-start = ((), (), s32[]{:S(2)}) async-start(), calls=%async_computation.6 | async-start | bytes 2097152 | tf_op jit(solution)/shard_map/psum | solution.py:103
  568.8 3.3 copy-start.9
  568.8 3.5 copy-start.6
  579.3 6.3 copy-start.5
  593.8 89.5 %copy-start.7 = (f32[2048,128]{0,1:T(8,128)S(1)}, f32[2048,128]{0,1:T(8,128)}, u32[]{:S(2)}) copy-start(f32[2048,128]{0,1:T(8,128)} %multiply_add_fusion.2) | copy-start | bytes 3145732
  683.3 5.5 copy-start.1
Sparse Core Ops, SparseCore 0:
  53.4 200.6 all-reduce.7
  257.7 86.4 all-reduce.5
  368.7 86.2 all-reduce.9
  482.6 86.2 all-reduce.11
  593.9 86.2 all-reduce.13
where the time goes:
time: 702 us; the launch traced here: 696 us
  waiting for transfers between devices  510 us (73%)
  matrix products  80.1 us (11%)
  local copies, waits for them, and re-layouts  48.6 us (7%)
  blocking collectives  20.4 us (3%)
  other arithmetic  15.5 us (2%)
  between operations  14.4 us (2%)
    psum x3, waiting for transfers between devices, apply_whole(): return lax.psum(tile_terms(vector), 'col') + extra(vector)  259 us
    psum x1, waiting for transfers between devices, shards(): residual = lax.psum(start_terms, 'col') - extra(user_factors)  90.1 us
    psum x1, waiting for transfers between devices, shards(): lax.psum(jnp.dot(item_factors.T, item_factors, precision=HIGHEST, preferr...  81.8 us
    all_to_all x1, waiting for transfers between devices, shards(): lax.all_to_all(served, ('row', 'col'), split_axis=0, concat_axis=0, tiled...  79.1 us
    dot_general x4, matrix products, tile_terms(): jnp.einsum('tuk,tik->tui', picked_users, item_tiles, precision=HIGHEST)  23.5 us
    all_to_all x1, blocking collectives, shards(): lax.all_to_all(wanted, ('row', 'col'), split_axis=0, concat_axis=0, tiled...  20.4 us
  transfers between devices with their start and end apart: 6, of which 6 were waited for; matrix products, arithmetic and copies ran while one was open for 6% of the time, Pallas kernels for 0%

commit v1 on v0

--- a/solution.py
+++ b/solution.py
@@ -102,7 +102,7 @@
     def apply_whole(vector):
         return lax.psum(tile_terms(vector), "col") + extra(vector)
 
-    residual = lax.psum(start_terms, "col") - extra(user_factors)
+    residual = lax.all_gather(start_terms, "col").sum(axis=0) - extra(user_factors)
     solved = conjugate(user_factors, residual, apply_whole)
     return solved
 

time: 702 us -> 747 us (1.064)
  waiting for transfers between devices: 510 us -> 538 us
  other arithmetic: 15.5 us -> 27.4 us
    all_gather x0 -> x1, waiting for transfers between devices: none -> 117 us  [shards(): lax.all_gather(start_terms, 'col').sum(axis=0) - extra(user_factors)]
    psum x1 -> x0, waiting for transfers between devices: 90.1 us -> none  [shards(): residual = lax.psum(start_terms, 'col') - extra(user_factors)]
    reduce_sum x0 -> x1, other arithmetic: none -> 7.65 us  [shards(): lax.all_gather(start_terms, 'col').sum(axis=0) - extra(user_factors)]
  transfers between devices with their start and end apart: 6 -> 6, of which waited for: 6 -> 6; matrix products, arithmetic and copies ran while one was open for 6% -> 4% of each run, Pallas kernels for 0% -> 0%
where the time goes in v1:
time: 747 us; the launch traced here: 741 us
  waiting for transfers between devices  538 us (72%)
  matrix products  81.6 us (11%)
  local copies, waits for them, and re-layouts  51.4 us (7%)
  other arithmetic  27.4 us (4%)
  blocking collectives  20.4 us (3%)
  between operations  15.8 us (2%)
    psum x3, waiting for transfers between devices, apply_whole(): return lax.psum(tile_terms(vector), 'col') + extra(vector)  259 us
    all_gather x1, waiting for transfers between devices, shards(): lax.all_gather(start_terms, 'col').sum(axis=0) - extra(user_factors)  117 us
    all_to_all x1, waiting for transfers between devices, shards(): lax.all_to_all(served, ('row', 'col'), split_axis=0, concat_axis=0, tiled...  81 us
    psum x1, waiting for transfers between devices, shards(): lax.psum(jnp.dot(item_factors.T, item_factors, precision=HIGHEST, preferr...  80.5 us
    dot_general x4, matrix products, tile_terms(): jnp.einsum('tuk,tik->tui', picked_users, item_tiles, precision=HIGHEST)  23.5 us
    all_to_all x1, blocking collectives, shards(): lax.all_to_all(wanted, ('row', 'col'), split_axis=0, concat_axis=0, tiled...  20.4 us
  transfers between devices with their start and end apart: 6, of which 6 were waited for; matrix products, arithmetic and copies ran while one was open for 4% of the time, Pallas kernels for 0%

profile of v1, /device:TPU:0, one launch (start us, length us, event | category | flops | bytes accessed | tf_op | source)
XLA Modules:
  0.0 740.8 jit_solution(10976611587351090543)
XLA Ops:
  8.2 20.4 %all_to_all.20 = s32[128,1,1]{2,1,0:T(1,128)S(1)} all-to-all(s32[128,1,1]{2,1,0:T(1,128)S(1)} %copy.49), channel_id=1, replica_groups=mesh['row'=8,'col'=16] {'row','col'}, dimensions={0} | all-to-all | bytes 1024 | tf_op jit(solution)/shard_map/all_to_all | solution.py:46
  31.0 4.3 gather_fusion
  35.3 7.2 bitcast_select_fusion
  42.5 6.1 all-to-all-start.1
  51.6 8.1 %fusion = f32[32,128,128]{2,1,0:T(8,128)} fusion(f32[32,512]{1,0:T(8,128)S(1)} %get-tuple-element.11, s32[32,512]{1,0:T(8,128)S(1)} %bitcast.99, s32[32,512]{1,0:T(8,128)S(1)} %bitcast.101), kind=kOutput, calls=%fused_computation.7 | convolution fusion | flops 3227516928 | bytes 2293760 | tf_op jit(solution)/shard_map/tnu,tni->tui/dot_general | solution.py:70
  59.6 8.2 %fusion.2 = f32[32,128,128]{2,1,0:T(8,128)} fusion(s32[32,512]{1,0:T(8,128)S(1)} %bitcast.100, f32[32,512]{1,0:T(8,128)S(1)} %get-tuple-element.10, s32[32,512]{1,0:T(8,128)S(1)} %bitcast.102), kind=kOutput, calls=%fused_computation.10 | convolution fusion | flops 3227516928 | bytes 2293760 | tf_op jit(solution)/shard_map/tnu,tni->tui/dot_general | solution.py:73
  67.9 81.0 %all-to-all-done.1 = f32[128,1,128,128]{3,2,1,0:T(8,128)} async-done(((f32[128,1,128,128]{3,2,1,0:T(8,128)}), f32[128,1,128,128]{3,2,1,0:T(8,128)}, u32[]{:S(2)}, u32[]{:S(2)}) %all-to-all-start.1) | async-done | bytes 8388640 | tf_op jit(solution)/shard_map/all_to_all | solution.py:48
  148.8 4.1 gather_fusion.1
  152.9 3.9 fusion.50
  156.9 4.6 fusion.28
  173.7 116.8 %all-gather.2.cloned.1.call-done = f32[16,2048,128]{2,1,0:T(8,128)} async-done(((f32[1,2048,128]{2,1,0:T(8,128)}), f32[16,2048,128]{2,1,0:T(8,128)}) %all-gather.2.cloned.1.call-update) | async-done | bytes 16777232 | tf_op jit(solution)/shard_map/all_gather | solution.py:105
  290.5 7.6 %reduce_sum.63 = f32[2048,128]{1,0:T(8,128)} reduce(f32[16,2048,128]{2,1,0:T(8,128)} %all-gather.2.cloned.1.call-done, f32[]{:T(128)} %constant.33.clone.1), dimensions={0}, to_apply=%region_0.0 | reduce | flops 3932160 | bytes 17825796 | tf_op jit(solution)/shard_map/reduce_sum | solution.py:105
  300.7 80.5 %all-reduce.5.cloned.1.call-done = f32[128,128]{1,0:T(8,128)} async-done(((f32[128,128]{1,0:T(8,128)}), f32[128,128]{1,0:T(8,128)}) %all-reduce.5.cloned.1.call-update) | async-done | bytes 65552 | tf_op jit(solution)/shard_map/psum | solution.py:51
  381.2 4.0 fusion.13
  387.7 3.2 gather_fusion.3
  391.0 6.3 fusion.26
  397.3 3.6 fusion.34
  400.9 3.5 copy.68
  408.2 86.7 %all-reduce.7.cloned.1.call-done = f32[2048,128]{0,1:T(8,128)} async-done(((f32[2048,128]{0,1:T(8,128)}), f32[2048,128]{0,1:T(8,128)}) %all-reduce.7.cloned.1.call-update) | async-done | bytes 1048592 | tf_op jit(solution)/shard_map/psum | solution.py:103
  495.0 3.1 multiply_reduce_fusion.3
  504.4 3.2 gather_fusion.4
  507.6 6.3 fusion.24
  513.9 3.6 fusion.32
  517.5 3.1 copy.71
  524.6 86.2 %all-reduce.9.cloned.1.call-done = f32[2048,128]{0,1:T(8,128)} async-done(((f32[2048,128]{0,1:T(8,128)}), f32[2048,128]{0,1:T(8,128)}) %all-reduce.9.cloned.1.call-update) | async-done | bytes 1048592 | tf_op jit(solution)/shard_map/psum | solution.py:103
  610.8 3.1 multiply_reduce_fusion.1
  620.7 3.2 gather_fusion.5
  624.0 6.3 fusion.22
  630.3 3.6 fusion.30
  638.4 86.4 %all-reduce.11.cloned.1.call-done = f32[2048,128]{0,1:T(8,128)} async-done(((f32[2048,128]{0,1:T(8,128)}), f32[2048,128]{0,1:T(8,128)}) %all-reduce.11.cloned.1.call-update) | async-done | bytes 1048592 | tf_op jit(solution)/shard_map/psum | solution.py:103
  724.8 3.0 fusion.41
  727.9 3.0 multiply_add_fusion
  (87 shorter events, 50.5 us)
Async XLA Ops:
  7.4 23.6 %copy-start = (f32[1024,128]{1,0:T(8,128)S(1)}, f32[1024,128]{1,0:T(8,128)}, u32[]{:S(2)}) copy-start(f32[1024,128]{1,0:T(8,128)} %param.12) | copy-start | bytes 1572868
  42.5 6.8 copy-start.14
  42.5 6.8 copy-start.10
  42.5 106.3 %all-to-all-start.1 = ((f32[128,1,128,128]{3,2,1,0:T(8,128)}), f32[128,1,128,128]{3,2,1,0:T(8,128)}, u32[]{:S(2)}, u32[]{:S(2)}) async-start(f32[128,1,128,128]{3,2,1,0:T(8,128)} %bitcast_select_fusion), calls=%async_computation.1 | async-start | bytes 16777216 | tf_op jit(solution)/shard_map/all_to_all | solution.py:48
  48.6 241.9 %all-gather.2.cloned.1.call-start = ((), (), s32[]{:S(2)}) async-start(), calls=%async_computation.2 | async-start | bytes 17825792 | tf_op jit(solution)/shard_map/all_gather | solution.py:105
  49.4 2.0 copy-start.15
  49.4 2.1 copy-start.13
  49.4 2.2 copy-start.16
  49.4 2.2 copy-start.17
  152.9 4.0 copy-start.11
  156.9 4.6 copy-start.4
  169.4 211.9 %all-reduce.5.cloned.1.call-start = ((), (), s32[]{:S(2)}) async-start(), calls=%async_computation.3 | async-start | bytes 131072 | tf_op jit(solution)/shard_map/psum | solution.py:51
  171.1 323.9 %all-reduce.7.cloned.1.call-start = ((), (), s32[]{:S(2)}) async-start(), calls=%async_computation.4 | async-start | bytes 2097152 | tf_op jit(solution)/shard_map/psum | solution.py:103
  391.0 6.3 copy-start.5
  406.8 88.2 %copy-start.12 = (f32[128,128]{1,0:T(8,128)S(1)}, f32[128,128]{1,0:T(8,128)}, u32[]{:S(2)}) copy-start(f32[128,128]{1,0:T(8,128)} %all-reduce.5.cloned.1.call-done) | copy-start | bytes 196612
  408.2 202.7 %all-reduce.9.cloned.1.call-start = ((), (), s32[]{:S(2)}) async-start(), calls=%async_computation.5 | async-start | bytes 2097152 | tf_op jit(solution)/shard_map/psum | solution.py:103
  498.1 2.6 copy-start.2
  499.7 1.0 copy-start.9
  507.6 6.3 copy-start.6
  524.4 200.4 %all-reduce.11.cloned.1.call-start = ((), (), s32[]{:S(2)}) async-start(), calls=%async_computation.6 | async-start | bytes 2097152 | tf_op jit(solution)/shard_map/psum | solution.py:103
  624.0 6.3 copy-start.7
  638.4 89.5 %copy-start.3 = (f32[2048,128]{0,1:T(8,128)S(1)}, f32[2048,128]{0,1:T(8,128)}, u32[]{:S(2)}) copy-start(f32[2048,128]{0,1:T(8,128)} %fusion.13) | copy-start | bytes 3145732
  638.4 89.5 %copy-start.8 = (f32[2048,128]{0,1:T(8,128)S(1)}, f32[2048,128]{0,1:T(8,128)}, u32[]{:S(2)}) copy-start(f32[2048,128]{0,1:T(8,128)} %multiply_add_fusion.2) | copy-start | bytes 3145732
  727.9 5.6 copy-start.1
Sparse Core Ops, SparseCore 0:
  169.5 120.9 all-gather.1
  408.3 86.6 all-reduce.6
  524.5 86.2 all-reduce.8
  638.6 86.2 all-reduce.10
Sparse Core Ops, SparseCore 1:
  174.6 206.6 all-reduce.4
